TPU v7x, 32 devices: a whole 2x2x4 slice. The times are simulated.
32 devices in a mesh: row: 8 (over y, x, core), col: 4 (over z).
Axes of the slice: x: 2, y: 2, z: 4, core: 2. Of those that a mesh axis runs over, the one named last changes fastest.
Arguments:
- kernel: float32 [6, 4096, 2, 2048], P(None, 'row', None, 'col'), may hold values from 0 to 1, as said below
- jitter: float32 [2, 2048], P(None, 'col'), may hold values from 0.05 to 0.5
Outputs:
- factored: float32 [6, 4096, 2, 2048], P(None, 'row', None, 'col')
Inputs may be any that keep to these rules, and one draw needn't show every extreme that they name: kernel is the matrix of a positive definite kernel function evaluated at 24576 demonstration states (rows) and the first 4096 of them (columns); it equals 1 on the diagonal.
All inputs are finite; a program needn't handle non-finite values.
Results may differ from a plain program's by a relative error of at most 0.0003.
Values sent between devices are 32-bit elements; how exact they have to be, the bound alone decides.
A program may use at most 192 MiB of HBM per device.

v0:
```python
import jax
import jax.numpy as jnp
from jax import lax
from jax.sharding import PartitionSpec as P


def from_root(value, axis, source):
    kept = jnp.where(lax.axis_index(axis) == source, value, 0).astype(value.dtype)
    return lax.psum(kept, axis)


def body(kernel, jitter):
    row_cycles, tile_size, col_cycles, _ = kernel.shape
    row_count = lax.axis_size("row")
    col_count = lax.axis_size("col")
    row_index = lax.axis_index("row")
    col_index = lax.axis_index("col")
    row_tiles = jnp.arange(row_cycles, dtype=jnp.int32) * row_count + row_index
    col_tiles = jnp.arange(col_cycles, dtype=jnp.int32) * col_count + col_index
    inner_rows = lax.broadcasted_iota(jnp.int32, (tile_size, tile_size), 0)
    inner_cols = lax.broadcasted_iota(jnp.int32, (tile_size, tile_size), 1)
    global_rows = row_tiles[:, None, None, None] * tile_size + inner_rows[None, :, :1, None]
    global_cols = col_tiles[None, None, :, None] * tile_size + inner_cols[None, :1, None, :]
    shifted = jnp.where(global_rows == global_cols, kernel + jitter[None, None, :, :], kernel)

    def factor_of(slices, section):
        square = slices[section // col_count][section // row_count]
        sym = jnp.tril(square) + jnp.tril(square, -1).T
        return jnp.linalg.cholesky(sym)

    def solve_place(factor, column, section):
        flat = column.reshape(row_cycles * tile_size, tile_size)
        solved = lax.linalg.triangular_solve(
            factor, flat, left_side=False, lower=True, transpose_a=True
        )
        solved = solved.reshape(row_cycles, tile_size, tile_size)
        which = row_tiles[:, None, None]
        placed = jnp.where(which == section, factor[None, :, :], solved)
        return jnp.where(which < section, 0.0, placed)

    def panel_step(slices, section):
        root_row = section % row_count
        root_col = section % col_count
        factor = from_root(factor_of(slices, section), "row", root_row)
        panel = solve_place(factor, slices[section // col_count], section)
        panel = from_root(panel, "col", root_col)
        gathered = []
        for cycle in range(col_cycles):
            wanted = cycle * col_count + col_index
            source = lax.dynamic_index_in_dim(panel, wanted // row_count, 0, keepdims=False)
            gathered.append(from_root(source, "row", wanted % row_count))
        return (panel, jnp.stack(gathered))

    def update_all(slices, panel, across, section):
        flat = panel.reshape(row_cycles * tile_size, tile_size)
        product = jnp.dot(
            flat,
            across.reshape(col_cycles * tile_size, tile_size).T,
            precision=lax.Precision.HIGHEST,
            preferred_element_type=jnp.float32,
        )
        product = product.reshape(row_cycles, tile_size, col_cycles, tile_size)
        return [
            jnp.where(
                col_tiles[cycle] > section, slices[cycle] - product[:, :, cycle, :], slices[cycle]
            )
            for cycle in range(col_cycles)
        ]

    def place_column(slices, panel, section):
        return [
            jnp.where(col_tiles[cycle] == section, panel, slices[cycle])
            for cycle in range(col_cycles)
        ]

    slices = [shifted[:, :, cycle, :] for cycle in range(col_cycles)]
    panel_zero, across_zero = panel_step(slices, 0)
    slices = update_all(slices, panel_zero, across_zero, 0)
    slices = place_column(slices, panel_zero, 0)
    panel_one, across_one = panel_step(slices, 1)
    slices = update_all(slices, panel_one, across_one, 1)
    slices = place_column(slices, panel_one, 1)
    result = jnp.stack(slices, axis=2)
    return jnp.where(global_rows >= global_cols, result, 0.0)


def solution(mesh):
    in_specs = (P(None, "row", None, "col"), P(None, "col"))
    out_specs = P(None, "row", None, "col")
    return jax.shard_map(body, mesh=mesh, in_specs=in_specs, out_specs=out_specs, check_vma=False)
```

profile of v0, /device:TPU:26, one launch (start us, length us, event | category | flops | bytes accessed | tf_op | source)
XLA Modules:
  0.0 1193.7 jit_solution(6660534862127087482)
XLA Ops:
  6.7 7.7 add_select_fusion
  21.6 11.7 cholesky.286
  33.4 9.8 custom-call.27
  44.0 11.7 cholesky.305
  55.7 10.0 custom-call.28
  66.4 11.7 cholesky.326
  78.9 9.8 custom-call.29
  89.3 22.8 %cholesky.343 = f32[128,128]{1,0:T(8,128)S(1)} custom-call(f32[128,128]{1,0:T(8,128)S(1)} %convolution_subtract_fusion.9), custom_call_target="Cholesky" | custom-call | tf_op jit(solution)/shard_map/jit(cholesky)/cholesky | solution.py:29
  124.0 49.8 %all-reduce.10.cloned.1.call-done = f32[512,512]{1,0:T(8,128)} async-done(((f32[512,512]{1,0:T(8,128)}), f32[512,512]{1,0:T(8,128)}) %all-reduce.10.cloned.1.call-update) | async-done | bytes 1048592 | tf_op jit(solution)/shard_map/psum | solution.py:9
  175.3 7.4 while.4
  183.4 40.1 %custom-call.30 = f32[4,128,128]{1,2,0:T(8,128)S(1)} custom-call(f32[4,128,128]{2,1,0:T(8,128)} %copy-done.4), custom_call_target="InvertDiagBlocksLowerTriangular" | custom-call | tf_op jit(solution)/shard_map/triangular_solve/custom-call.3 | solution.py:33
  239.5 8.2 fusion.25
  266.0 220.8 %all-reduce.12.cloned.1.call-done = f32[6,512,512]{2,1,0:T(8,128)} async-done(((f32[6,512,512]{2,1,0:T(8,128)}), f32[6,512,512]{2,1,0:T(8,128)}) %all-reduce.12.cloned.1.call-update) | async-done | bytes 6291472 | tf_op jit(solution)/shard_map/psum | solution.py:9
  492.6 59.3 %all-reduce.20.cloned.1.call-done = (f32[1,512,512]{2,1,0:T(8,128)}, f32[1,512,512]{2,1,0:T(8,128)}) async-done(((f32[1,512,512]{2,1,0:T(8,128)}, f32[1,512,512]{2,1,0:T(8,128)}), (f32[1,512,512]{2,1,0:T(8,128)}, f32[1,512,512]{2,1,0:T(8,128)})) %all-reduce.20.cloned.1.call-update) | async-done | bytes 2097168 | tf_op jit(solution)/shard_map/psum | solution.py:9
  551.8 25.6 %fusion.8 = f32[6,512,2,512]{3,1,0,2:T(8,128)} fusion(f32[6,512,512]{2,1,0:T(8,128)} %all-reduce.12.cloned.1.call-done, f32[1,512,512]{2,1,0:T(8,128)} %get-tuple-element.41, f32[1,512,512]{2,1,0:T(8,128)} %get-tuple-element.42), kind=kOutput, calls=%fused_computation.25 | convolution fusion | flops 19327877120 | bytes 20971520 | tf_op jit(solution)/shard_map/dot_general | solution.py:56
  577.5 9.7 fusion
  590.9 11.7 cholesky.358
  603.3 9.8 custom-call.31
  613.9 12.1 %cholesky.377 = f32[128,128]{1,0:T(8,128)S(1)} custom-call(f32[128,128]{1,0:T(8,128)S(1)} %cholesky.443), custom_call_target="Cholesky" | custom-call | tf_op jit(solution)/shard_map/jit(cholesky)/cholesky | solution.py:29
  626.8 9.8 custom-call.32
  637.3 11.7 cholesky.398
  649.7 9.8 custom-call.33
  660.1 11.9 cholesky.415
  676.6 55.9 %all-reduce.14.cloned.1.call-done = f32[512,512]{1,0:T(8,128)} async-done(((f32[512,512]{1,0:T(8,128)}), f32[512,512]{1,0:T(8,128)}) %all-reduce.14.cloned.1.call-update) | async-done | bytes 1048592 | tf_op jit(solution)/shard_map/psum | solution.py:9
  734.0 8.2 while.5
  742.9 40.1 %custom-call.34 = f32[4,128,128]{1,2,0:T(8,128)S(1)} custom-call(f32[4,128,128]{2,1,0:T(8,128)} %copy-done.3), custom_call_target="InvertDiagBlocksLowerTriangular" | custom-call | tf_op jit(solution)/shard_map/triangular_solve/custom-call.3 | solution.py:33
  799.2 8.2 fusion.22
  825.5 220.9 %all-reduce.16.cloned.1.call-done = f32[6,512,512]{2,1,0:T(8,128)} async-done(((f32[6,512,512]{2,1,0:T(8,128)}), f32[6,512,512]{2,1,0:T(8,128)}) %all-reduce.16.cloned.1.call-update) | async-done | bytes 6291472 | tf_op jit(solution)/shard_map/psum | solution.py:9
  1053.4 58.0 %all-reduce.18.cloned.1.call-done = (f32[1,512,512]{2,1,0:T(8,128)}, f32[1,512,512]{2,1,0:T(8,128)}) async-done(((f32[1,512,512]{2,1,0:T(8,128)}, f32[1,512,512]{2,1,0:T(8,128)}), (f32[1,512,512]{2,1,0:T(8,128)}, f32[1,512,512]{2,1,0:T(8,128)})) %all-reduce.18.cloned.1.call-update) | async-done | bytes 2097168 | tf_op jit(solution)/shard_map/psum | solution.py:9
  1111.4 25.0 %fusion.6 = f32[6,512,2,512]{3,1,0,2:T(8,128)} fusion(f32[6,512,512]{2,1,0:T(8,128)} %all-reduce.16.cloned.1.call-done, f32[1,512,512]{2,1,0:T(8,128)} %get-tuple-element.39, f32[1,512,512]{2,1,0:T(8,128)} %get-tuple-element.40), kind=kOutput, calls=%fused_computation.23 | convolution fusion | flops 19327877120 | bytes 20971520 | tf_op jit(solution)/shard_map/dot_general | solution.py:56
  1136.4 19.8 %fusion.2 = (f32[6,512,1,512]{3,1,0,2:T(8,128)}, f32[6,512,1,512]{3,1,0,2:T(8,128)}) fusion(f32[6,512,512]{2,1,0:T(8,128)} %all-reduce.16.cloned.1.call-done, f32[6,512,512]{2,1,0:T(8,128)} %fusion, f32[6,512,2,512]{3,1,0,2:T(8,128)} %fusion.6, pred[]{:T(512)} %bitcast.41, pred[]{:T(512)} %bitcast.1, f32[6,512,512]{2,1,0:T(8,128)} %all-reduce.12.cloned.1.call-done, ...), kind=kLoop, calls=%fused_computation.12 | loop fusion | flops 14155776 | bytes 56623112 | tf_op jit(solution)/shard_map/stack | solution.py:83
  1161.6 25.1 %copy.17 = f32[6,512,2,512]{3,2,1,0:T(2,128)} copy(f32[6,512,2,512]{3,1,0,2:T(8,128)S(1)} %maximum_select_fusion) | data formatting | bytes 25165824 | tf_op jit(solution)/shard_map/jit(_where)/select_n | solution.py:84
  (148 shorter events, 130.4 us)
Async XLA Ops:
  6.5 167.3 %all-reduce.10.cloned.1.call-start = ((), (), s32[]{:S(2)}) async-start(), calls=%async_computation | async-start | bytes 2097152 | tf_op jit(solution)/shard_map/psum | solution.py:9
  14.4 4.8 copy-start
  117.1 369.7 %all-reduce.12.cloned.1.call-start = ((), (), s32[]{:S(2)}) async-start(), calls=%async_computation.1 | async-start | bytes 12582912 | tf_op jit(solution)/shard_map/psum | solution.py:9
  175.3 56.9 %slice-start.4 = ((s8[6291456]{0:T(1024)(128)(4,1)}), s8[2097152]{0:T(1024)(128)(4,1)S(1)}, s32[]{:S(2)}) async-start(s8[6291456]{0:T(1024)(128)(4,1)} %bitcast.183), calls=%async_computation.10 | async-start | bytes 4194304
  182.7 0.7 copy-start.4
  226.4 5.8 slice-start.5
  252.3 6.7 copy-start.1
  265.9 285.9 %all-reduce.20.cloned.1.call-start = ((), (), s32[]{:S(2)}) async-start(), calls=%async_computation.5 | async-start | bytes 4194304 | tf_op jit(solution)/shard_map/psum | solution.py:9
  490.1 242.5 %all-reduce.14.cloned.1.call-start = ((), (), s32[]{:S(2)}) async-start(), calls=%async_computation.2 | async-start | bytes 2097152 | tf_op jit(solution)/shard_map/psum | solution.py:9
  551.8 25.6 %slice-start = ((s8[6291456]{0:T(1024)(128)(4,1)}), s8[4194304]{0:T(1024)(128)(4,1)S(1)}, s32[]{:S(2)}) async-start(s8[6291456]{0:T(1024)(128)(4,1)} %bitcast.167), calls=%async_computation.6 | async-start | bytes 8388608
  551.8 25.6 %slice-start.1 = ((s8[6291456]{0:T(1024)(128)(4,1)}), s8[2097152]{0:T(1024)(128)(4,1)S(1)}, s32[]{:S(2)}) async-start(s8[6291456]{0:T(1024)(128)(4,1)} %bitcast.167), calls=%async_computation.7 | async-start | bytes 4194304
  676.6 369.8 %all-reduce.16.cloned.1.call-start = ((), (), s32[]{:S(2)}) async-start(), calls=%async_computation.3 | async-start | bytes 12582912 | tf_op jit(solution)/shard_map/psum | solution.py:9
  734.0 57.8 %slice-start.2 = ((s8[6291456]{0:T(1024)(128)(4,1)}), s8[2097152]{0:T(1024)(128)(4,1)S(1)}, s32[]{:S(2)}) async-start(s8[6291456]{0:T(1024)(128)(4,1)} %bitcast.171), calls=%async_computation.8 | async-start | bytes 4194304
  742.2 0.7 copy-start.3
  785.9 5.8 slice-start.3
  812.0 6.7 copy-start.2
  825.5 285.9 %all-reduce.18.cloned.1.call-start = ((), (), s32[]{:S(2)}) async-start(), calls=%async_computation.4 | async-start | bytes 4194304 | tf_op jit(solution)/shard_map/psum | solution.py:9
Sparse Core Ops, SparseCore 0:
  117.2 56.5 all-reduce.9
  266.0 220.7 all-reduce.11
  490.2 61.5 all-reduce.19
  676.7 55.8 all-reduce.13
  825.6 220.7 all-reduce.15
  1049.7 61.5 all-reduce.17
where the time goes:
time: 1200 us; the launch traced here: 1190 us
  waiting for transfers between devices  665 us (55%)
  other arithmetic  328 us (27%)
  matrix products  106 us (9%)
  local copies, waits for them, and re-layouts  69.6 us (6%)
  between operations  24.5 us (2%)
    psum x6, waiting for transfers between devices, from_root(): return lax.psum(kept, axis)  665 us
    another operation x29, other arithmetic, factor_of(): return jnp.linalg.cholesky(sym)  169 us
    another operation x7, other arithmetic, solve_place(): lax.linalg.triangular_solve(factor, flat, left_side=False, lower=True, tr...  88.8 us
    another operation x14, matrix products, solve_place(): lax.linalg.triangular_solve(factor, flat, left_side=False, lower=True, tr...  51.6 us
    dot_general x2, matrix products, update_all(): jnp.dot(flat, across.reshape(col_cycles * tile_size, tile_size).T, precis...  50.6 us
    another operation x29, local copies, waits for them, and re-layouts, solve_place(): lax.linalg.triangular_solve(factor, flat, left_side=False, lower=True, tr...  28.8 us
    select_n x1, local copies, waits for them, and re-layouts, body(): return jnp.where(global_rows >= global_cols, result, 0.0)  25.1 us
  transfers between devices with their start and end apart: 6, of which 6 were waited for; matrix products, arithmetic and copies ran while one was open for 1% of the time, Pallas kernels for 0%

commit v1 on v0

v1 whole, which is shorter than its diff:
```python
import functools

import jax
import jax.numpy as jnp
from jax import lax
from jax.experimental import pallas as pl
from jax.experimental.pallas import tpu as pltpu
from jax.sharding import PartitionSpec as P

BLOCK = 128
SUB = 8


def eliminate(square):
    groups = BLOCK // SUB
    rows = lax.broadcasted_iota(jnp.int32, (SUB, BLOCK), 0)
    lanes = lax.broadcasted_iota(jnp.int32, (SUB, BLOCK), 1)
    left = [square[g * SUB : (g + 1) * SUB, :] for g in range(groups)]
    right = [jnp.where(lanes == rows + g * SUB, 1.0, 0.0).astype(jnp.float32) for g in range(groups)]
    for k in range(BLOCK):
        home, inner = divmod(k, SUB)
        pivot = 1.0 / left[home][inner : inner + 1, k : k + 1]
        row_left = left[home][inner : inner + 1, :] * pivot
        row_right = right[home][inner : inner + 1, :] * pivot
        for g in range(home, groups):
            column = left[g][:, k : k + 1]
            if g == home:
                column = jnp.where(rows[:, :1] > inner, column, 0.0)
            left[g] = left[g] - column * row_left
            right[g] = right[g] - column * row_right
    done = []
    for g in range(groups):
        diagonal = jnp.sum(
            jnp.where(lanes == rows + g * SUB, left[g], 0.0), axis=1, keepdims=True
        )
        done.append(right[g] / jnp.sqrt(diagonal))
    return jnp.concatenate(done, axis=0)


def factor_kernel(lead_ref, inverse_ref, work_ref):
    size = lead_ref.shape[0]
    count = size // BLOCK
    width = size + BLOCK

    def start(i, carry):
        here = pl.ds(pl.multiple_of(i * BLOCK, BLOCK), BLOCK)
        work_ref[here, :size] = lead_ref[here, :]
        row = lax.broadcasted_iota(jnp.int32, (BLOCK, size), 0) + i * BLOCK
        lane = lax.broadcasted_iota(jnp.int32, (BLOCK, size), 1)
        work_ref[here, size:] = jnp.where(row == lane, 1.0, 0.0).astype(jnp.float32)
        return carry

    lax.fori_loop(0, count, start, 0)

    def step(k, carry):
        offset = pl.multiple_of(k * BLOCK, BLOCK)
        here = pl.ds(offset, BLOCK)
        window = pl.ds(offset, width)
        inverse = eliminate(work_ref[here, here])
        panel = jnp.dot(
            inverse, work_ref[here, window],
            precision=lax.Precision.HIGHEST, preferred_element_type=jnp.float32,
        )
        work_ref[here, window] = panel

        def reduce(i, carry):
            there = pl.ds(pl.multiple_of(i * BLOCK, BLOCK), BLOCK)
            product = lax.dot_general(
                work_ref[here, there], work_ref[here, window], (((0,), (0,)), ((), ())),
                precision=lax.Precision.HIGHEST, preferred_element_type=jnp.float32,
            )
            work_ref[there, window] = work_ref[there, window] - product
            return carry

        lax.fori_loop(k + 1, count, reduce, 0)
        return carry

    lax.fori_loop(0, count, step, 0)
    inverse_ref[...] = work_ref[:, size:]


def inverse_factor(lead):
    size = lead.shape[0]
    return pl.pallas_call(
        factor_kernel,
        out_shape=jax.ShapeDtypeStruct((size, size), jnp.float32),
        in_specs=[pl.BlockSpec(memory_space=pltpu.VMEM)],
        out_specs=pl.BlockSpec(memory_space=pltpu.VMEM),
        scratch_shapes=[pltpu.VMEM((size, 2 * size), jnp.float32)],
        compiler_params=pltpu.CompilerParams(vmem_limit_bytes=40 * 2**20),
        cost_estimate=pl.CostEstimate(
            flops=100_000_000_000, bytes_accessed=8 * size * size, transcendentals=0
        ),
        name="inverse_factor",
    )(lead)


DELAY = 2


def relay(own, col_count, col_index, before_step, first_free):
    cycles = len(own)
    order = [(1, 0), (1, 1)] if cycles > 1 else [(1, 0)]
    sent = [0, len(order)]
    while len(order) < 2 * cycles:
        turn = 0 if sent[0] < cycles and (order[-1][0] == 1 or sent[1] == cycles) else 1
        if turn == 0 and len(order) <= sent[0]:
            turn = 1
        order.append((turn, sent[turn]))
        sent[turn] += 1
    when = {item: step for step, item in enumerate(order)}
    steps = len(order) + DELAY * (col_count - 3)
    back = [lax.ppermute(own[a], "col", [(1, 0)]) for a in range(cycles)]
    got = []
    for step in range(steps):
        pairs = []
        value = None
        if step < cycles:
            value = own[step]
            pairs.append((0, 1))
        if step < len(order):
            panel, a = order[step]
            mine = own[a] if panel == 1 else got[a]
            value = mine if value is None else jnp.where(col_index == 1, mine, value)
            if col_count > 2:
                pairs.append((1, 2))
        passing = [c for c in range(2, col_count - 1) if 0 <= step - DELAY * (c - 1) < len(order)]
        if passing:
            before = got[step - DELAY]
            value = before if value is None else jnp.where(col_index >= 2, before, value)
            pairs.extend((c, c + 1) for c in passing)
        if step == first_free:
            value, _ = lax.optimization_barrier((value, before_step))
        got.append(lax.ppermute(value, "col", pairs))

    def found(panel, a):
        choices = [own[a] if panel == 0 else back[a], got[a] if panel == 0 else own[a]]
        choices += [got[when[panel, a] + DELAY * (c - 2)] for c in range(2, col_count)]
        value = choices[-1]
        for c in range(col_count - 2, -1, -1):
            value = jnp.where(col_index == c, choices[c], value)
        return value

    return [jnp.concatenate([found(0, a), found(1, a)], axis=1) for a in range(cycles)]


def times_transposed(left, right, precision):
    return lax.dot_general(
        left, right, (((1,), (1,)), ((), ())),
        precision=precision, preferred_element_type=jnp.float32,
    )


def body(kernel, jitter):
    row_cycles, tile, col_cycles, _ = kernel.shape
    row_count = lax.axis_size("row")
    col_count = lax.axis_size("col")
    row_index = lax.axis_index("row")
    col_index = lax.axis_index("col")
    rows = lax.broadcasted_iota(jnp.int32, (tile, tile), 0)
    cols = lax.broadcasted_iota(jnp.int32, (tile, tile), 1)
    slices = [kernel[:, :, cycle, :] for cycle in range(col_cycles)]

    def jittered(value, cycle, row_tile, col_tile):
        on = (rows == cols) & (row_tile == col_tile)
        return value + jnp.where(on, jitter[cycle][None, :], 0.0)

    def symmetric(square):
        return jnp.tril(square) + jnp.tril(square, -1).T

    corner = jittered(slices[0][0], 0, row_index, col_index)
    places = ((0, 0), (1, 0), (1, 1))
    kept = jnp.stack(
        [jnp.where((row_index == i) & (col_index == j), corner, 0.0) for i, j in places]
    )
    corner_sum = lax.psum(kept, ("row", "col"))
    first, below, second = corner_sum
    first, second = symmetric(first), symmetric(second)
    lead = jnp.concatenate(
        [jnp.concatenate([first, below.T], axis=1), jnp.concatenate([below, second], axis=1)], axis=0
    )
    inverse = inverse_factor(lead)

    raw = relay([slices[0][a] for a in range(row_cycles)], col_count, col_index, corner_sum, 2)

    wanted = [cycle * col_count + col_index for cycle in range(col_cycles)]
    kept = []
    for cycle in range(col_cycles):
        source = raw[0]
        for a in range(1, -(-(cycle + 1) * col_count // row_count)):
            source = jnp.where(wanted[cycle] // row_count == a, raw[a], source)
        kept.append(jnp.where(wanted[cycle] % row_count == row_index, source, 0.0))
    across = lax.psum(jnp.concatenate(kept, axis=0), "row")
    across = times_transposed(across, inverse, lax.Precision.HIGHEST)

    outs = []
    for a in range(row_cycles):
        row_tile = a * row_count + row_index
        rows_a = raw[a]
        if a == 0:
            rows_a = jnp.where(
                row_index == 0, lead[:tile], jnp.where(row_index == 1, lead[tile:], rows_a)
            )
        panel = times_transposed(rows_a, inverse, lax.Precision.HIGHEST)
        update = times_transposed(panel, across, lax.Precision.HIGH)
        parts = []
        for cycle in range(col_cycles):
            col_tile = wanted[cycle]
            value = jittered(slices[cycle][a], cycle, row_tile, col_tile)
            value = value - update[:, cycle * tile : (cycle + 1) * tile]
            if cycle == 0:
                value = jnp.where(col_index == 0, panel[:, :tile], value)
                value = jnp.where(col_index == 1, panel[:, tile:], value)
            keep = row_tile * tile + rows >= col_tile * tile + cols
            parts.append(jnp.where(keep, value, 0.0))
        outs.append(jnp.stack(parts, axis=1))
    return jnp.stack(outs, axis=0)


def solution(mesh):
    in_specs = (P(None, "row", None, "col"), P(None, "col"))
    out_specs = P(None, "row", None, "col")
    return jax.shard_map(body, mesh=mesh, in_specs=in_specs, out_specs=out_specs, check_vma=False)
```

time: 1200 us -> 666 us (0.56)
  waiting for transfers between devices: 665 us -> 278 us
  other arithmetic: 328 us -> 57.2 us
  Pallas kernels: 0 us -> 112 us
  starting transfers between devices: 0.21 us -> 29.8 us
  matrix products: 106 us -> 86.4 us
    psum x6 -> x2, waiting for transfers between devices: 665 us -> 133 us  [the longest x1 133 us: body(): corner_sum = lax.psum(kept, ('row', 'col'))]
    another operation x37 -> x8, other arithmetic: 278 us -> 6.09 us  [the longest x6 2.56 us: body(): outs.append(jnp.stack(parts, axis=1))]
    ppermute x0 -> x20, waiting for transfers between devices: none -> 145 us  [the longest x14 145 us: relay(): got.append(lax.ppermute(value, 'col', pairs))]
    pallas_call x0 -> x1, Pallas kernels: none -> 112 us  [inverse_factor(): pl.pallas_call(factor_kernel, out_shape=jax.ShapeDtypeStruct((size, size)...]
    another operation x26 -> x0, matrix products: 55.4 us -> none  [the longest x14 51.6 us: solve_place(): lax.linalg.triangular_solve(factor, flat, left_side=False, lower=True, tr...]
    dot_general x2 -> x13, matrix products: 50.6 us -> 86.4 us  [times_transposed(): lax.dot_general(left, right, (((1,), (1,)), ((), ())), precision=precisio...]
    ppermute x0 -> x20, starting transfers between devices: none -> 29.8 us  [the longest x14 19.8 us: relay(): got.append(lax.ppermute(value, 'col', pairs))]
    select_n x2 -> x0, local copies, waits for them, and re-layouts: 25.4 us -> none  [the longest x1 25.1 us: body(): return jnp.where(global_rows >= global_cols, result, 0.0)]
  transfers between devices with their start and end apart: 6 -> 22, of which waited for: 6 -> 11; matrix products, arithmetic and copies ran while one was open for 1% -> 18% of each run, Pallas kernels for 0% -> 17%
where the time goes in v1:
time: 666 us; the launch traced here: 657 us
  waiting for transfers between devices  278 us (42%)
  Pallas kernels  112 us (17%)
  matrix products  86.4 us (13%)
  local copies, waits for them, and re-layouts  79.4 us (12%)
  other arithmetic  57.2 us (9%)
  starting transfers between devices  29.8 us (4%)
  between operations  14.5 us (2%)
    ppermute x14, waiting for transfers between devices, relay(): got.append(lax.ppermute(value, 'col', pairs))  145 us
    psum x1, waiting for transfers between devices, body(): corner_sum = lax.psum(kept, ('row', 'col'))  133 us
    pallas_call x1, Pallas kernels, inverse_factor(): pl.pallas_call(factor_kernel, out_shape=jax.ShapeDtypeStruct((size, size)...  112 us
    dot_general x13, matrix products, times_transposed(): lax.dot_general(left, right, (((1,), (1,)), ((), ())), precision=precisio...  86.4 us
    another operation x1, local copies, waits for them, and re-layouts, body(): return jnp.stack(outs, axis=0)  22 us
    ppermute x14, starting transfers between devices, relay(): got.append(lax.ppermute(value, 'col', pairs))  19.8 us
    slice x1, local copies, waits for them, and re-layouts, body(): value = jittered(slices[cycle][a], cycle, row_tile, col_tile)  19.5 us
    select_n x4, other arithmetic, found(): value = jnp.where(col_index == c, choices[c], value)  17.6 us
  transfers between devices with their start and end apart: 22, of which 11 were waited for; matrix products, arithmetic and copies ran while one was open for 18% of the time, Pallas kernels for 17%

profile of v1, /device:TPU:26, one launch (start us, length us, event | category | flops | bytes accessed | tf_op | source)
XLA Modules:
  0.0 656.9 jit_solution(11046373365978364162)
XLA Ops:
  6.5 19.5 %fusion.96 = (f32[1,512,1,512]{3,2,1,0:T(1,128)}, f32[1,512,1,512]{3,2,1,0:T(1,128)}, f32[1,512,1,512]{3,2,1,0:T(1,128)}, f32[1,512,1,512]{3,2,1,0:T(1,128)}, f3...) fusion(f32[6,512,2,512]{3,2,1,0:T(2,128)} %param.2), kind=kLoop, calls=%fused_computation.177 | loop fusion | bytes 25165824 | tf_op jit(solution)/shard_map/slice | solution.py:209
  40.0 3.7 select_select_fusion.11
  43.7 132.7 %all-reduce.3.cloned.1.call-done = f32[3,512,512]{1,2,0:T(8,128)} async-done(((f32[3,512,512]{1,2,0:T(8,128)}), f32[3,512,512]{1,2,0:T(8,128)}) %all-reduce.3.cloned.1.call-update) | async-done | bytes 3145744 | tf_op jit(solution)/shard_map/psum | solution.py:176
  179.3 22.2 %collective-permute-done.1 = f32[512,512]{1,0:T(8,128)S(1)} collective-permute-done((f32[512,512]{1,0:T(8,128)}, f32[512,512]{1,0:T(8,128)S(1)}, u32[]{:S(2)}, u32[]{:S(2)}) %collective-permute-start.1) | collective-permute-done | bytes 1048608 | tf_op jit(solution)/shard_map/ppermute | solution.py:134
  207.3 23.9 %collective-permute-done.3 = f32[512,512]{1,0:T(8,128)} collective-permute-done((f32[512,512]{1,0:T(8,128)}, f32[512,512]{1,0:T(8,128)}, u32[]{:S(2)}, u32[]{:S(2)}) %collective-permute-start.3) | collective-permute-done | bytes 1048608 | tf_op jit(solution)/shard_map/ppermute | solution.py:134
  231.2 4.1 select_select_fusion.14
  236.7 16.8 %collective-permute-done.7 = f32[512,512]{1,0:T(8,128)S(1)} collective-permute-done((f32[512,512]{1,0:T(8,128)}, f32[512,512]{1,0:T(8,128)S(1)}, u32[]{:S(2)}, u32[]{:S(2)}) %collective-permute-start.7) | collective-permute-done | bytes 1048608 | tf_op jit(solution)/shard_map/ppermute | solution.py:134
  253.5 19.0 %collective-permute-done.5 = f32[512,512]{1,0:T(8,128)S(1)} collective-permute-done((f32[512,512]{1,0:T(8,128)S(1)}, f32[512,512]{1,0:T(8,128)S(1)}, u32[]{:S(2)}, u32[]{:S(2)}) %collective-permute-start.5) | collective-permute-done | bytes 1048608 | tf_op jit(solution)/shard_map/ppermute | solution.py:134
  272.5 4.1 select_select_fusion.12
  290.5 10.6 %collective-permute-done.8 = f32[512,512]{1,0:T(8,128)} collective-permute-done((f32[512,512]{1,0:T(8,128)}, f32[512,512]{1,0:T(8,128)}, u32[]{:S(2)}, u32[]{:S(2)}) %collective-permute-start.8) | collective-permute-done | bytes 1048608 | tf_op jit(solution)/shard_map/ppermute | solution.py:134
  311.0 4.2 slice_bitcast_fusion.1
  317.8 9.0 %collective-permute-done.11 = f32[512,512]{1,0:T(8,128)} collective-permute-done((f32[512,512]{1,0:T(8,128)}, f32[512,512]{1,0:T(8,128)}, u32[]{:S(2)}, u32[]{:S(2)}) %collective-permute-start.11) | collective-permute-done | bytes 1048608 | tf_op jit(solution)/shard_map/ppermute | solution.py:134
  349.8 3.8 collective-permute-done.10
  357.4 111.5 %inverse_factor.1 = f32[1024,1024]{1,0:T(8,128)S(1)} custom-call(f32[1024,1024]{1,0:T(8,128)S(1)} %copy-done.2), custom_call_target="tpu_custom_call" | custom-call | flops 99999997952 | bytes 8388608 | tf_op jit(solution)/shard_map/inverse_factor/pallas_call | solution.py:84
  469.1 8.2 %fusion = f32[512,1024]{1,0:T(8,128)} fusion(f32[1024,1024]{1,0:T(8,128)S(1)} %inverse_factor.1, f32[512,512]{1,0:T(8,128)S(1)} %copy-done.25, f32[512,512]{1,0:T(8,128)S(1)} %copy-done.29, f32[512,512]{1,0:T(8,128)S(1)} %copy-done.27, f32[512,512]{1,0:T(8,128)S(1)} %copy-done.31, f32[512,512]{1,0:T(8,128)S(1)} %copy-done.23, f32[512,512]{1,0:T(8,128)S(1)} %copy-done.21, ...), kind=kOutput, calls=%fused_computation.4 | convolution fusion | flops 6445072384 | bytes 12582914 | tf_op jit(solution)/shard_map/dot_general | solution.py:148
  477.3 8.5 %fusion.6 = f32[512,1024]{1,0:T(8,128)} fusion(f32[1024,1024]{1,0:T(8,128)S(1)} %inverse_factor.1, f32[512,512]{1,0:T(8,128)S(1)} %copy-done.44, f32[512,512]{1,0:T(8,128)S(1)} %copy-done.43), kind=kOutput, calls=%fused_computation.13 | convolution fusion | flops 6442975232 | bytes 8388608 | tf_op jit(solution)/shard_map/dot_general | solution.py:148
  489.4 17.5 %fusion.98 = f32[1024,1024]{1,0:T(8,128)S(1)} fusion(f32[1024,1024]{1,0:T(8,128)} %all-reduce.5.cloned.1.call-done, f32[1024,1024]{1,0:T(8,128)} %copy-done), kind=kOutput, calls=%fused_computation.179 | convolution fusion | flops 12884901888 | bytes 12582912 | tf_op jit(solution)/shard_map/dot_general | solution.py:148
  506.9 3.7 fusion.99
  519.4 3.7 fusion.100
  526.6 18.2 %collective-permute-done.17 = f32[512,512]{1,0:T(8,128)S(1)} collective-permute-done((f32[512,512]{1,0:T(8,128)S(1)}, f32[512,512]{1,0:T(8,128)S(1)}, u32[]{:S(2)}, u32[]{:S(2)}) %collective-permute-start.17) | collective-permute-done | bytes 1048608 | tf_op jit(solution)/shard_map/ppermute | solution.py:134
  546.2 7.0 %fusion.11 = f32[512,1024]{1,0:T(8,128)S(1)} fusion(f32[1024,1024]{1,0:T(8,128)S(1)} %copy-done.1, f32[512,512]{1,0:T(8,128)S(1)} %get-tuple-element.54, f32[512,512]{1,0:T(8,128)S(1)} %get-tuple-element.55), kind=kOutput, calls=%fused_computation.19 | convolution fusion | flops 6442975232 | bytes 8388608 | tf_op jit(solution)/shard_map/dot_general | solution.py:148
  553.2 3.7 fusion.101
  558.9 8.3 %collective-permute-done.14 = f32[512,512]{1,0:T(8,128)S(1)} collective-permute-done((f32[512,512]{1,0:T(8,128)}, f32[512,512]{1,0:T(8,128)S(1)}, u32[]{:S(2)}, u32[]{:S(2)}) %collective-permute-start.14) | collective-permute-done | bytes 1048608 | tf_op jit(solution)/shard_map/ppermute | solution.py:134
  568.2 13.6 %collective-permute-done.18 = f32[512,512]{1,0:T(8,128)} collective-permute-done((f32[512,512]{1,0:T(8,128)S(1)}, f32[512,512]{1,0:T(8,128)}, u32[]{:S(2)}, u32[]{:S(2)}) %collective-permute-start.18) | collective-permute-done | bytes 1048608 | tf_op jit(solution)/shard_map/ppermute | solution.py:134
  581.8 5.9 select_select_fusion.2
  587.7 8.5 %fusion.26 = f32[512,1024]{1,0:T(8,128)S(1)} fusion(f32[1024,1024]{1,0:T(8,128)S(1)} %copy-done.1, f32[512,512]{1,0:T(8,128)} %get-tuple-element.38, f32[512,512]{1,0:T(8,128)} %get-tuple-element.37), kind=kOutput, calls=%fused_computation.37 | convolution fusion | flops 6442975232 | bytes 8388608 | tf_op jit(solution)/shard_map/dot_general | solution.py:148
  596.3 4.2 fusion.104
  600.5 6.9 %fusion.21 = f32[512,1024]{1,0:T(8,128)S(1)} fusion(f32[1024,1024]{1,0:T(8,128)S(1)} %copy-done.1, f32[512,512]{1,0:T(8,128)S(1)} %get-tuple-element.50, f32[512,512]{1,0:T(8,128)S(1)} %copy-done.45), kind=kOutput, calls=%fused_computation.31 | convolution fusion | flops 6442975232 | bytes 8388608 | tf_op jit(solution)/shard_map/dot_general | solution.py:148
  607.4 3.7 fusion.103
  611.1 7.1 %fusion.16 = f32[512,1024]{1,0:T(8,128)S(1)} fusion(f32[1024,1024]{1,0:T(8,128)S(1)} %copy-done.1, f32[512,512]{1,0:T(8,128)S(1)} %get-tuple-element.51, f32[512,512]{1,0:T(8,128)S(1)} %copy-done.46), kind=kOutput, calls=%fused_computation.25 | convolution fusion | flops 6442975232 | bytes 8388608 | tf_op jit(solution)/shard_map/dot_general | solution.py:148
  618.3 3.7 fusion.102
  627.9 22.0 %copy.24 = f32[6,512,2,512]{3,2,1,0:T(2,128)} copy(f32[6,512,2,512]{3,1,2,0:T(8,128)} %fusion.30) | data formatting | bytes 25165824 | tf_op jit(solution)/shard_map/stack | solution.py:217
  (198 shorter events, 102.9 us)
Async XLA Ops:
  6.5 169.8 %all-reduce.3.cloned.1.call-start = ((), (), s32[]{:S(2)}) async-start(), calls=%async_computation | async-start | bytes 6291456 | tf_op jit(solution)/shard_map/psum | solution.py:176
  26.1 300.7 %copy-start.3 = (f32[1,512,1,512]{3,2,1,0:T(1,128)}, f32[1,512,1,512]{3,2,1,0:T(1,128)S(1)}, u32[]{:S(2)}) copy-start(f32[1,512,1,512]{3,2,1,0:T(1,128)S(1)} %get-tuple-element.13) | copy-start | bytes 3145732
  33.1 456.2 %all-reduce.5.cloned.1.call-start = ((), (), s32[]{:S(2)}) async-start(), calls=%async_computation.1 | async-start | bytes 8388608 | tf_op jit(solution)/shard_map/psum | solution.py:193
  35.5 4.5 collective-permute-start
  38.2 1.7 collective-permute-start.2
  176.4 25.1 %collective-permute-start.1 = (f32[512,512]{1,0:T(8,128)}, f32[512,512]{1,0:T(8,128)S(1)}, u32[]{:S(2)}, u32[]{:S(2)}) collective-permute-start(f32[512,512]{1,0:T(8,128)} %get-tuple-element.6), channel_id=1, source_target_pairs={{0,1},{1,2},{2,3},{4,5},{5,6},{6,7},{8,9},{9,10},{10,11},{12,13},{... | collective-permute-start | bytes 3145736 | tf_op jit(solution)/shard_map/ppermute | solution.py:134
  177.7 29.6 %collective-permute-start.4 = (f32[512,512]{1,0:T(8,128)}, f32[512,512]{1,0:T(8,128)}, u32[]{:S(2)}, u32[]{:S(2)}) collective-permute-start(f32[512,512]{1,0:T(8,128)} %bitcast.200), channel_id=1, source_target_pairs={{1,0},{5,4},{9,8},{13,12},{17,16},{21,20},{25,24},{29,28}} | collective-permute-start | bytes 3145736 | tf_op jit(solution)/shard_map/ppermute | solution.py:113
  202.9 28.3 %collective-permute-start.3 = (f32[512,512]{1,0:T(8,128)}, f32[512,512]{1,0:T(8,128)}, u32[]{:S(2)}, u32[]{:S(2)}) collective-permute-start(f32[512,512]{1,0:T(8,128)} %select_select_fusion.15), channel_id=1, source_target_pairs={{0,1},{1,2},{2,3},{4,5},{5,6},{6,7},{8,9},{9,10},{10,11},{12,13},{... | collective-permute-start | bytes 3145736 | tf_op jit(solution)/shard_map/ppermute | solution.py:134
  204.2 32.6 %collective-permute-start.6 = (f32[512,512]{1,0:T(8,128)}, f32[512,512]{1,0:T(8,128)}, u32[]{:S(2)}, u32[]{:S(2)}) collective-permute-start(f32[512,512]{1,0:T(8,128)} %bitcast.198), channel_id=1, source_target_pairs={{1,0},{5,4},{9,8},{13,12},{17,16},{21,20},{25,24},{29,28}} | collective-permute-start | bytes 3145736 | tf_op jit(solution)/shard_map/ppermute | solution.py:113
  205.9 66.7 %copy-start.12 = (f32[1,512,1,512]{3,2,1,0:T(1,128)S(1)}, f32[1,512,1,512]{3,2,1,0:T(1,128)}, u32[]{:S(2)}) copy-start(f32[1,512,1,512]{3,2,1,0:T(1,128)} %get-tuple-element.16) | copy-start | bytes 3145732
  205.9 47.7 %collective-permute-start.7 = (f32[512,512]{1,0:T(8,128)}, f32[512,512]{1,0:T(8,128)S(1)}, u32[]{:S(2)}, u32[]{:S(2)}) collective-permute-start(f32[512,512]{1,0:T(8,128)} %get-tuple-element.56), channel_id=1, source_target_pairs={{0,1},{1,2},{2,3},{4,5},{5,6},{6,7},{8,9},{9,10},{10,11},{12,13},{... | collective-permute-start | bytes 3145736 | tf_op jit(solution)/shard_map/ppermute | solution.py:134
  235.3 42.6 %copy-start.7 = (f32[1,512,1,512]{3,2,1,0:T(1,128)S(1)}, f32[1,512,1,512]{3,2,1,0:T(1,128)}, u32[]{:S(2)}) copy-start(f32[1,512,1,512]{3,2,1,0:T(1,128)} %get-tuple-element.17) | copy-start | bytes 3145732
  235.3 37.2 %collective-permute-start.5 = (f32[512,512]{1,0:T(8,128)S(1)}, f32[512,512]{1,0:T(8,128)S(1)}, u32[]{:S(2)}, u32[]{:S(2)}) collective-permute-start(f32[512,512]{1,0:T(8,128)S(1)} %get-tuple-element.44), channel_id=1, source_target_pairs={{1,2},{2,3},{5,6},{6,7},{9,10},{10,11},{13,14},{14,15},{17,18},{18... | collective-permute-start | bytes 3145736 | tf_op jit(solution)/shard_map/ppermute | solution.py:134
  276.6 24.5 %collective-permute-start.8 = (f32[512,512]{1,0:T(8,128)}, f32[512,512]{1,0:T(8,128)}, u32[]{:S(2)}, u32[]{:S(2)}) collective-permute-start(f32[512,512]{1,0:T(8,128)} %get-tuple-element.43), channel_id=1, source_target_pairs={{1,2},{2,3},{5,6},{6,7},{9,10},{10,11},{13,14},{14,15},{17,18},{18... | collective-permute-start | bytes 3145736 | tf_op jit(solution)/shard_map/ppermute | solution.py:134
  278.9 232.2 %collective-permute-start.9 = (f32[512,512]{1,0:T(8,128)}, f32[512,512]{1,0:T(8,128)}, u32[]{:S(2)}, u32[]{:S(2)}) collective-permute-start(f32[512,512]{1,0:T(8,128)} %bitcast.199), channel_id=1, source_target_pairs={{1,0},{5,4},{9,8},{13,12},{17,16},{21,20},{25,24},{29,28}} | collective-permute-start | bytes 3145736 | tf_op jit(solution)/shard_map/ppermute | solution.py:113
  281.6 277.3 %collective-permute-start.12 = (f32[512,512]{1,0:T(8,128)}, f32[512,512]{1,0:T(8,128)}, u32[]{:S(2)}, u32[]{:S(2)}) collective-permute-start(f32[512,512]{1,0:T(8,128)} %bitcast.196), channel_id=1, source_target_pairs={{1,0},{5,4},{9,8},{13,12},{17,16},{21,20},{25,24},{29,28}} | collective-permute-start | bytes 3145736 | tf_op jit(solution)/shard_map/ppermute | solution.py:113
  284.4 274.5 %collective-permute-start.15 = (f32[512,512]{1,0:T(8,128)}, f32[512,512]{1,0:T(8,128)}, u32[]{:S(2)}, u32[]{:S(2)}) collective-permute-start(f32[512,512]{1,0:T(8,128)} %bitcast.197), channel_id=1, source_target_pairs={{1,0},{5,4},{9,8},{13,12},{17,16},{21,20},{25,24},{29,28}} | collective-permute-start | bytes 3145736 | tf_op jit(solution)/shard_map/ppermute | solution.py:113
  287.1 271.8 %collective-permute-start.19 = (f32[512,512]{1,0:T(8,128)}, f32[512,512]{1,0:T(8,128)}, u32[]{:S(2)}, u32[]{:S(2)}) collective-permute-start(f32[512,512]{1,0:T(8,128)} %bitcast.195), channel_id=1, source_target_pairs={{1,0},{5,4},{9,8},{13,12},{17,16},{21,20},{25,24},{29,28}} | collective-permute-start | bytes 3145736 | tf_op jit(solution)/shard_map/ppermute | solution.py:113
  303.5 23.3 %collective-permute-start.11 = (f32[512,512]{1,0:T(8,128)}, f32[512,512]{1,0:T(8,128)}, u32[]{:S(2)}, u32[]{:S(2)}) collective-permute-start(f32[512,512]{1,0:T(8,128)} %broadcast_select_fusion.6), channel_id=1, source_target_pairs={{1,2},{2,3},{5,6},{6,7},{9,10},{10,11},{13,14},{14,15},{17,18},{18... | collective-permute-start | bytes 3145736 | tf_op jit(solution)/shard_map/ppermute | solution.py:134
  330.3 23.3 %collective-permute-start.10 = (f32[512,512]{1,0:T(8,128)}, f32[512,512]{1,0:T(8,128)S(1)}, u32[]{:S(2)}, u32[]{:S(2)}) collective-permute-start(f32[512,512]{1,0:T(8,128)} %get-tuple-element.40), channel_id=1, source_target_pairs={{0,1},{1,2},{2,3},{4,5},{5,6},{6,7},{8,9},{9,10},{10,11},{12,13},{... | collective-permute-start | bytes 3145736 | tf_op jit(solution)/shard_map/ppermute | solution.py:134
  353.6 115.4 %copy-start.16 = (f32[512,512]{1,0:T(8,128)}, f32[512,512]{1,0:T(8,128)S(1)}, u32[]{:S(2)}) copy-start(f32[512,512]{1,0:T(8,128)S(1)} %collective-permute-done.10) | copy-start | bytes 3145732
  353.8 132.0 %collective-permute-start.13 = (f32[512,512]{1,0:T(8,128)S(1)}, f32[512,512]{1,0:T(8,128)S(1)}, u32[]{:S(2)}, u32[]{:S(2)}) collective-permute-start(f32[512,512]{1,0:T(8,128)S(1)} %broadcast_select_fusion.5), channel_id=1, source_target_pairs={{1,2},{2,3},{5,6},{6,7},{9,10},{10,11},{13,14},{14,15},{17,18},{18... | collective-permute-start | bytes 3145736 | tf_op jit(solution)/shard_map/ppermute | solution.py:134
  357.4 111.6 %copy-start.21 = (f32[512,512]{1,0:T(8,128)S(1)}, f32[512,512]{1,0:T(8,128)}, u32[]{:S(2)}) copy-start(f32[512,512]{1,0:T(8,128)} %get-tuple-element.19) | copy-start | bytes 3145732
  357.4 111.6 %copy-start.23 = (f32[512,512]{1,0:T(8,128)S(1)}, f32[512,512]{1,0:T(8,128)}, u32[]{:S(2)}) copy-start(f32[512,512]{1,0:T(8,128)} %get-tuple-element.20) | copy-start | bytes 3145732
  357.4 111.6 %copy-start.25 = (f32[512,512]{1,0:T(8,128)S(1)}, f32[512,512]{1,0:T(8,128)}, u32[]{:S(2)}) copy-start(f32[512,512]{1,0:T(8,128)} %get-tuple-element.22) | copy-start | bytes 3145732
  357.4 111.6 %copy-start.27 = (f32[512,512]{1,0:T(8,128)S(1)}, f32[512,512]{1,0:T(8,128)}, u32[]{:S(2)}) copy-start(f32[512,512]{1,0:T(8,128)} %copy-done.26) | copy-start | bytes 3145732
  357.4 111.6 %copy-start.29 = (f32[512,512]{1,0:T(8,128)S(1)}, f32[512,512]{1,0:T(8,128)}, u32[]{:S(2)}) copy-start(f32[512,512]{1,0:T(8,128)} %copy.7) | copy-start | bytes 3145732
  357.4 111.6 %copy-start.31 = (f32[512,512]{1,0:T(8,128)S(1)}, f32[512,512]{1,0:T(8,128)}, u32[]{:S(2)}) copy-start(f32[512,512]{1,0:T(8,128)} %copy.12) | copy-start | bytes 3145732
  488.0 23.1 %collective-permute-start.16 = (f32[512,512]{1,0:T(8,128)}, f32[512,512]{1,0:T(8,128)}, u32[]{:S(2)}, u32[]{:S(2)}) collective-permute-start(f32[512,512]{1,0:T(8,128)} %broadcast_select_fusion.4), channel_id=1, source_target_pairs={{1,2},{2,3},{5,6},{6,7},{9,10},{10,11},{13,14},{14,15},{17,18},{18... | collective-permute-start | bytes 3145736 | tf_op jit(solution)/shard_map/ppermute | solution.py:134
  515.8 29.0 %collective-permute-start.17 = (f32[512,512]{1,0:T(8,128)S(1)}, f32[512,512]{1,0:T(8,128)S(1)}, u32[]{:S(2)}, u32[]{:S(2)}) collective-permute-start(f32[512,512]{1,0:T(8,128)S(1)} %get-tuple-element.53), channel_id=1, source_target_pairs={{1,2},{2,3},{5,6},{6,7},{9,10},{10,11},{13,14},{14,15},{17,18},{18... | collective-permute-start | bytes 3145736 | tf_op jit(solution)/shard_map/ppermute | solution.py:134
  525.2 42.1 %collective-permute-start.14 = (f32[512,512]{1,0:T(8,128)}, f32[512,512]{1,0:T(8,128)S(1)}, u32[]{:S(2)}, u32[]{:S(2)}) collective-permute-start(f32[512,512]{1,0:T(8,128)} %collective-permute-done.11), channel_id=1, source_target_pairs={{2,3},{6,7},{10,11},{14,15},{18,19},{22,23},{26,27},{30,31}} | collective-permute-start | bytes 3145736 | tf_op jit(solution)/shard_map/ppermute | solution.py:134
  544.8 37.0 %collective-permute-start.18 = (f32[512,512]{1,0:T(8,128)S(1)}, f32[512,512]{1,0:T(8,128)}, u32[]{:S(2)}, u32[]{:S(2)}) collective-permute-start(f32[512,512]{1,0:T(8,128)S(1)} %collective-permute-done.17), channel_id=1, source_target_pairs={{2,3},{6,7},{10,11},{14,15},{18,19},{22,23},{26,27},{30,31}} | collective-permute-start | bytes 3145736 | tf_op jit(solution)/shard_map/ppermute | solution.py:134
  (47 other events, 271.8 us)
Sparse Core Ops, SparseCore 0:
  33.2 143.1 all-reduce.2
  349.9 82.9 all-reduce.4
